TPU v7x, 32 devices: a whole 2x2x4 slice. The times are simulated.
32 devices in a mesh: dp: 2 (over x), expert: 16 (over z, y, core).
Axes of the slice: x: 2, y: 2, z: 4, core: 2. Of those that a mesh axis runs over, the one named last changes fastest.
Arguments:
- tokens: bfloat16 [4096, 1024], P(('dp', 'expert')), may hold values from -6 to 6
- routes: int32 [4096, 6], P(('dp', 'expert')), may hold values from 0 to 15, all different within a row; in each aligned block of 128 rows (0 to 127, 128 to 255, ...) at most 96 rows name the same one
- route_weights: float32 [4096, 6], P(('dp', 'expert')), may hold values from 0.1 to 1
- gate_weight: bfloat16 [16, 1024, 512], P('expert'), may hold values from -0.1875 to 0.1875
- up_weight: bfloat16 [16, 1024, 512], P('expert'), may hold values from -0.1875 to 0.1875
- down_weight: bfloat16 [16, 512, 1024], P('expert'), may hold values from -0.25 to 0.25
- cotangent: bfloat16 [4096, 1024], P(('dp', 'expert')), may hold values from -3 to 3
Outputs:
- mixed_latent: bfloat16 [4096, 1024], P(('dp', 'expert'))
- latent_grad: bfloat16 [4096, 1024], P(('dp', 'expert'))
- gate_grad: float32 [16, 1024, 512], P('expert', 'dp')
- up_grad: float32 [16, 1024, 512], P('expert', 'dp')
- down_grad: float32 [16, 512, 1024], P('expert', None, 'dp')
Inputs may be any that keep to these rules, and one draw needn't show every extreme that they name: `routes`: each row names 6 different experts. In each aligned block of 128 rows (the rows of one device) no expert is named by more than 96 rows, and some expert is named by exactly 96 rows in some block.
All inputs are finite; a program needn't handle non-finite values.
Results may differ from a plain program's by a relative error of at most 0.015.
Values may be sent and summed in bfloat16 or wider, within the bound.
A program may use at most 64 MiB of HBM per device.

v0:
```python
import jax
import jax.numpy as jnp
from jax import lax
from jax.sharding import PartitionSpec as P


def slot_plan(route_rows, experts, capacity):
    flat_routes = route_rows.reshape(-1)
    one_hot = (flat_routes[:, None] == jnp.arange(experts, dtype=jnp.int32)[None, :]).astype(
        jnp.int32
    )
    earlier = jnp.cumsum(one_hot, axis=0) - one_hot
    slot_rank = jnp.sum(earlier * one_hot, axis=1)
    kept_mask = slot_rank < capacity
    slot_index = jnp.where(kept_mask, flat_routes * capacity + slot_rank, experts * capacity)
    return (kept_mask, slot_index)


def pack_rows(row_values, slot_index, experts, capacity):
    latent_width = row_values.shape[1]
    buffer = jnp.zeros((experts * capacity + 1, latent_width), row_values.dtype)
    buffer = buffer.at[slot_index].set(row_values)
    return buffer[:-1].reshape(experts, capacity, latent_width)


def unpack_rows(buffer, slot_index, top_count):
    latent_width = buffer.shape[-1]
    padded = jnp.concatenate(
        [buffer.reshape(-1, latent_width), jnp.zeros((1, latent_width), buffer.dtype)], axis=0
    )
    return padded[slot_index].reshape(-1, top_count, latent_width)


def expert_forward(inputs, gate_matrix, up_matrix, down_matrix):
    gate_pre = jnp.dot(inputs, gate_matrix, preferred_element_type=jnp.float32)
    up_pre = jnp.dot(inputs, up_matrix, preferred_element_type=jnp.float32)
    hidden = (jax.nn.silu(gate_pre) * up_pre).astype(jnp.bfloat16)
    outputs = jnp.dot(hidden, down_matrix, preferred_element_type=jnp.float32).astype(jnp.bfloat16)
    return (outputs, gate_pre, up_pre, hidden)


def expert_backward(out_grads, gate_pre, up_pre, gate_matrix, up_matrix, down_matrix):
    contract_last = (((1,), (1,)), ((), ()))
    hidden_grad = lax.dot_general(
        out_grads, down_matrix, contract_last, preferred_element_type=jnp.float32
    )
    sigmoid_gate = jax.nn.sigmoid(gate_pre)
    up_grad_pre = (hidden_grad * gate_pre * sigmoid_gate).astype(jnp.bfloat16)
    gate_grad_pre = (
        hidden_grad * up_pre * sigmoid_gate * (1.0 + gate_pre * (1.0 - sigmoid_gate))
    ).astype(jnp.bfloat16)
    input_grads = lax.dot_general(
        gate_grad_pre, gate_matrix, contract_last, preferred_element_type=jnp.float32
    )
    input_grads = input_grads + lax.dot_general(
        up_grad_pre, up_matrix, contract_last, preferred_element_type=jnp.float32
    )
    return (input_grads.astype(jnp.bfloat16), gate_grad_pre, up_grad_pre)


def shards(tokens, routes, route_weights, gate_weight, up_weight, down_weight, cotangent):
    token_count, latent_width = tokens.shape
    top_count = routes.shape[1]
    experts = lax.axis_size("expert")
    capacity = token_count * top_count // experts
    kept_mask, slot_index = slot_plan(routes, experts, capacity)
    kept_weights = route_weights * kept_mask.reshape(token_count, top_count).astype(jnp.float32)
    send_tokens = pack_rows(jnp.repeat(tokens, top_count, axis=0), slot_index, experts, capacity)
    grad_rows = (kept_weights[:, :, None] * cotangent[:, None, :].astype(jnp.float32)).astype(
        jnp.bfloat16
    )
    send_grads = pack_rows(
        grad_rows.reshape(token_count * top_count, latent_width), slot_index, experts, capacity
    )
    gate_matrix = gate_weight[0]
    up_matrix = up_weight[0]
    down_matrix = down_weight[0]
    inbox_tokens = lax.all_to_all(send_tokens, "expert", split_axis=0, concat_axis=0, tiled=True)
    inputs = inbox_tokens.reshape(-1, latent_width)
    outputs, gate_pre, up_pre, hidden = expert_forward(inputs, gate_matrix, up_matrix, down_matrix)
    returned_outputs = lax.all_to_all(
        outputs.reshape(experts, capacity, latent_width),
        "expert",
        split_axis=0,
        concat_axis=0,
        tiled=True,
    )
    inbox_grads = lax.all_to_all(send_grads, "expert", split_axis=0, concat_axis=0, tiled=True)
    out_grads = inbox_grads.reshape(-1, latent_width)
    input_grads, gate_grad_pre, up_grad_pre = expert_backward(
        out_grads, gate_pre, up_pre, gate_matrix, up_matrix, down_matrix
    )
    returned_grads = lax.all_to_all(
        input_grads.reshape(experts, capacity, latent_width),
        "expert",
        split_axis=0,
        concat_axis=0,
        tiled=True,
    )
    mixed_latent = jnp.sum(
        unpack_rows(returned_outputs, slot_index, top_count).astype(jnp.float32)
        * kept_weights[:, :, None],
        axis=1,
    ).astype(jnp.bfloat16)
    latent_grad = jnp.sum(
        unpack_rows(returned_grads, slot_index, top_count).astype(jnp.float32), axis=1
    ).astype(jnp.bfloat16)
    contract_rows = (((0,), (0,)), ((), ()))
    pair_grads = jnp.concatenate([gate_grad_pre, up_grad_pre], axis=1)
    ffn_width = hidden.shape[1]
    window = inputs
    pair_share = lax.psum_scatter(
        lax.dot_general(
            window, pair_grads, contract_rows, preferred_element_type=jnp.float32
        ).astype(jnp.bfloat16),
        "dp",
        scatter_dimension=0,
        tiled=True,
    ).astype(jnp.float32)
    window = out_grads
    down_share = lax.psum_scatter(
        lax.dot_general(window, hidden, contract_rows, preferred_element_type=jnp.float32).astype(
            jnp.bfloat16
        ),
        "dp",
        scatter_dimension=0,
        tiled=True,
    ).astype(jnp.float32)
    gate_grad = pair_share[:, :ffn_width][None]
    up_grad = pair_share[:, ffn_width:][None]
    down_grad = down_share.T[None]
    return (mixed_latent, latent_grad, gate_grad, up_grad, down_grad)


def solution(mesh):
    placed = (
        P(("dp", "expert"), None),
        P(("dp", "expert"), None),
        P(("dp", "expert"), None),
        P("expert", None, None),
        P("expert", None, None),
        P("expert", None, None),
        P(("dp", "expert"), None),
    )
    return jax.shard_map(
        shards,
        mesh=mesh,
        in_specs=placed,
        out_specs=(
            P(("dp", "expert"), None),
            P(("dp", "expert"), None),
            P("expert", "dp", None),
            P("expert", "dp", None),
            P("expert", None, "dp"),
        ),
        check_vma=False,
    )
```

profile of v0, /device:TPU:1, one launch (start us, length us, event | category | flops | bytes accessed | tf_op | source)
XLA Modules:
  0.0 224.6 jit_solution(15422988846847013577)
XLA Ops:
  14.2 6.8 %scatter_custom_fusion = bf16[769,1024]{1,0:T(8,128)(2,1)S(1)} fusion(s32[768]{0:T(1024)S(1)} %fusion.22, bf16[768,1024]{1,0:T(8,128)(2,1)} %reshape.138, bf16[]{:T(256)} %constant.7.clone.1), kind=kCustom, calls=%fused_computation.33 | custom fusion | bytes 1575424 | tf_op jit(solution)/shard_map/scatter | solution.py:22
  22.3 7.5 %all-to-all-start = ((bf16[16,48,1024]{2,1,0:T(8,128)(2,1)}), bf16[16,48,1024]{2,1,0:T(8,128)(2,1)}, u32[]{:S(2)}, u32[]{:S(2)}) async-start(bf16[16,48,1024]{2,1,0:T(8,128)(2,1)} %bitcast.62), calls=%async_computation | async-start | bytes 3145728 | tf_op jit(solution)/shard_map/all_to_all | solution.py:78
  30.2 2.5 %mul.80 = f32[128,6,1024]{2,1,0:T(8,128)} broadcast(bf16[128,1024]{1,0:T(8,128)(2,1)S(1)} %copy-done.5), dimensions={0,2} | broadcast | bytes 3407872 | tf_op jit(solution)/shard_map/mul | solution.py:69
  32.7 4.8 %mul.81 = f32[768,1024]{1,0:T(8,128)} reshape(f32[128,6,1024]{2,1,0:T(8,128)} %mul.80) | data formatting | bytes 6291456 | tf_op jit(solution)/shard_map/mul | solution.py:69
  37.5 10.1 %scatter_custom_fusion.1 = bf16[769,1024]{1,0:T(8,128)(2,1)S(1)} fusion(s32[768]{0:T(1024)S(1)} %fusion.22, f32[768,1024]{1,0:T(8,128)} %mul.81, f32[768]{0:T(1024)S(1)} %mul.78, bf16[]{:T(256)} %constant.7.clone.1), kind=kCustom, calls=%fused_computation.9 | custom fusion | flops 1572864 | bytes 4724738 | tf_op jit(solution)/shard_map/scatter | solution.py:22
  48.9 13.4 %all-to-all-done = bf16[16,48,1024]{2,1,0:T(8,128)(2,1)} async-done(((bf16[16,48,1024]{2,1,0:T(8,128)(2,1)}), bf16[16,48,1024]{2,1,0:T(8,128)(2,1)}, u32[]{:S(2)}, u32[]{:S(2)}) %all-to-all-start) | async-done | bytes 1572896 | tf_op jit(solution)/shard_map/all_to_all | solution.py:78
  62.2 8.8 %all-to-all-start.2 = ((bf16[16,48,1024]{2,1,0:T(8,128)(2,1)}), bf16[16,48,1024]{2,1,0:T(8,128)(2,1)S(1)}, u32[]{:S(2)}, u32[]{:S(2)}) async-start(bf16[16,48,1024]{2,1,0:T(8,128)(2,1)} %bitcast.63), calls=%async_computation.2 | async-start | bytes 3145728 | tf_op jit(solution)/shard_map/all_to_all | solution.py:88
  71.2 4.0 %fusion.13 = f32[768,512]{0,1:T(8,128)} fusion(bf16[768,1024]{1,0:T(8,128)(2,1)} %bitcast.2, bf16[1,1024,512]{2,1,0:T(8,128)(2,1)} %param.10), kind=kOutput, calls=%fused_computation.29 | convolution fusion | flops 805306368 | bytes 4194304 | tf_op jit(solution)/shard_map/dot_general | solution.py:35
  75.2 3.6 %fusion.9 = f32[768,512]{0,1:T(8,128)} fusion(bf16[768,1024]{1,0:T(8,128)(2,1)} %bitcast.2, bf16[1,1024,512]{2,1,0:T(8,128)(2,1)S(1)} %copy-done.2), kind=kOutput, calls=%fused_computation.25 | convolution fusion | flops 805306368 | bytes 4194304 | tf_op jit(solution)/shard_map/dot_general | solution.py:36
  78.8 24.5 %all-to-all-done.2 = bf16[16,48,1024]{2,1,0:T(8,128)(2,1)S(1)} async-done(((bf16[16,48,1024]{2,1,0:T(8,128)(2,1)}), bf16[16,48,1024]{2,1,0:T(8,128)(2,1)S(1)}, u32[]{:S(2)}, u32[]{:S(2)}) %all-to-all-start.2) | async-done | bytes 1572896 | tf_op jit(solution)/shard_map/all_to_all | solution.py:88
  103.3 4.4 %multiply_convert_fusion.2 = (bf16[768,512]{0,1:T(8,128)(2,1)}, bf16[768,512]{0,1:T(8,128)(2,1)S(1)}, bf16[768,512]{0,1:T(8,128)(2,1)S(1)}) fusion(f32[768,512]{0,1:T(8,128)} %fusion.13, f32[768,512]{0,1:T(8,128)} %fusion.9, bf16[768,1024]{1,0:T(8,128)(2,1)S(1)} %bitcast.67, bf16[1,512,1024]{2,1,0:T(8,128)(2,1)S(1)} %copy-done), kind=kOutput, calls=%fused_computation.13 | convolution fusion | flops 811597824 | bytes 8126464 | tf_op jit(solution)/shard_map/dot_general | solution.py:44
  107.7 2.7 %fusion.11 = f32[768,1024]{1,0:T(8,128)} fusion(bf16[768,512]{0,1:T(8,128)(2,1)S(1)} %get-tuple-element.16, bf16[1,1024,512]{2,1,0:T(8,128)(2,1)S(1)} %copy-done.4), kind=kOutput, calls=%fused_computation.27 | convolution fusion | flops 805306368 | bytes 4980736 | tf_op jit(solution)/shard_map/dot_general | solution.py:52
  113.6 4.4 %add_convert_fusion = bf16[768,1024]{1,0:T(8,128)(2,1)} fusion(f32[768,1024]{1,0:T(8,128)} %fusion.11, bf16[768,512]{0,1:T(8,128)(2,1)} %get-tuple-element.15, bf16[1,1024,512]{2,1,0:T(8,128)(2,1)S(1)} %copy-done.3), kind=kOutput, calls=%fused_computation.5 | convolution fusion | flops 806879232 | bytes 6553600 | tf_op jit(solution)/shard_map/dot_general | solution.py:55
  118.0 8.8 %all-to-all-start.3 = ((bf16[16,48,1024]{2,1,0:T(8,128)(2,1)}), bf16[16,48,1024]{2,1,0:T(8,128)(2,1)S(1)}, u32[]{:S(2)}, u32[]{:S(2)}) async-start(bf16[16,48,1024]{2,1,0:T(8,128)(2,1)} %bitcast.65), calls=%async_computation.3 | async-start | bytes 3145728 | tf_op jit(solution)/shard_map/all_to_all | solution.py:93
  126.8 4.8 %convolution_convert_fusion = bf16[1024,1024]{1,0:T(8,128)(2,1)} fusion(bf16[768,1024]{1,0:T(8,128)(2,1)} %bitcast.2, bf16[768,512]{0,1:T(8,128)(2,1)} %get-tuple-element.15, bf16[768,512]{0,1:T(8,128)(2,1)S(1)} %get-tuple-element.16), kind=kOutput, calls=%fused_computation.7 | convolution fusion | flops 1614807040 | bytes 5242880 | tf_op jit(solution)/shard_map/dot_general | solution.py:113
  134.9 24.2 %all-to-all-done.3 = bf16[16,48,1024]{2,1,0:T(8,128)(2,1)S(1)} async-done(((bf16[16,48,1024]{2,1,0:T(8,128)(2,1)}), bf16[16,48,1024]{2,1,0:T(8,128)(2,1)S(1)}, u32[]{:S(2)}, u32[]{:S(2)}) %all-to-all-start.3) | async-done | bytes 1572896 | tf_op jit(solution)/shard_map/all_to_all | solution.py:93
  160.2 8.8 %all-to-all-start.1 = ((bf16[16,48,1024]{2,1,0:T(8,128)(2,1)}), bf16[16,48,1024]{2,1,0:T(8,128)(2,1)}, u32[]{:S(2)}, u32[]{:S(2)}) async-start(bf16[16,48,1024]{2,1,0:T(8,128)(2,1)} %bitcast.66), calls=%async_computation.1 | async-start | bytes 3145728 | tf_op jit(solution)/shard_map/all_to_all | solution.py:81
  173.1 3.6 %gather_fusion.1 = bf16[768,1024]{1,0:T(8,128)(2,1)} fusion(bf16[769,1024]{1,0:T(8,128)(2,1)S(1)} %concatenate.10, s32[1024]{0:T(1024)S(1)} %pad_clamp_fusion), kind=kCustom, calls=%fused_computation.1 | custom fusion | bytes 3148800 | tf_op jit(solution)/shard_map/gather | solution.py:31
  176.6 2.5 %reshape.115 = bf16[128,6,1024]{2,1,0:T(8,128)(2,1)S(1)} reshape(bf16[768,1024]{1,0:T(8,128)(2,1)} %gather_fusion.1) | data formatting | bytes 3145728 | tf_op jit(solution)/shard_map/reshape | solution.py:31
  179.1 2.2 reduce_sum.35
  181.3 20.1 %all-to-all-done.1 = bf16[16,48,1024]{2,1,0:T(8,128)(2,1)} async-done(((bf16[16,48,1024]{2,1,0:T(8,128)(2,1)}), bf16[16,48,1024]{2,1,0:T(8,128)(2,1)}, u32[]{:S(2)}, u32[]{:S(2)}) %all-to-all-start.1) | async-done | bytes 1572896 | tf_op jit(solution)/shard_map/all_to_all | solution.py:81
  203.0 3.6 %gather_fusion = bf16[768,1024]{1,0:T(8,128)(2,1)} fusion(bf16[769,1024]{1,0:T(8,128)(2,1)S(1)} %concatenate.9, s32[1024]{0:T(1024)S(1)} %pad_clamp_fusion), kind=kCustom, calls=%fused_computation | custom fusion | bytes 3148800 | tf_op jit(solution)/shard_map/gather | solution.py:31
  206.5 3.9 %reshape.116 = f32[128,6,1024]{2,1,0:T(8,128)} reshape(bf16[768,1024]{1,0:T(8,128)(2,1)} %gather_fusion) | data formatting | bytes 4718592 | tf_op jit(solution)/shard_map/convert_element_type | solution.py:101
  210.4 4.3 %multiply_reduce_fusion = bf16[128,1024]{1,0:T(8,128)(2,1)} fusion(f32[128,6,1024]{2,1,0:T(8,128)} %reshape.116, f32[128,6]{1,0:T(8,128)S(1)} %broadcast_select_fusion), kind=kLoop, calls=%fused_computation.4 | loop fusion | flops 1441792 | bytes 3410944 | tf_op jit(solution)/shard_map/reduce_sum | solution.py:100
  (54 shorter events, 26.4 us)
Async XLA Ops:
  7.2 96.2 %copy-start = (bf16[1,512,1024]{2,1,0:T(8,128)(2,1)S(1)}, bf16[1,512,1024]{2,1,0:T(8,128)(2,1)}, u32[]{:S(2)}) copy-start(bf16[1,512,1024]{2,1,0:T(8,128)(2,1)} %param.12) | copy-start | bytes 3145732
  22.3 7.7 %copy-start.6 = (f32[128,6]{0,1:T(8,128)S(1)}, f32[128,6]{0,1:T(8,128)}, u32[]{:S(2)}) copy-start(f32[128,6]{0,1:T(8,128)} %param.9) | copy-start | bytes 9220
  22.3 7.9 %copy-start.5 = (bf16[128,1024]{1,0:T(8,128)(2,1)S(1)}, bf16[128,1024]{1,0:T(8,128)(2,1)}, u32[]{:S(2)}) copy-start(bf16[128,1024]{1,0:T(8,128)(2,1)} %param.13) | copy-start | bytes 786436
  22.3 39.9 %all-to-all-start = ((bf16[16,48,1024]{2,1,0:T(8,128)(2,1)}), bf16[16,48,1024]{2,1,0:T(8,128)(2,1)}, u32[]{:S(2)}, u32[]{:S(2)}) async-start(bf16[16,48,1024]{2,1,0:T(8,128)(2,1)} %bitcast.62), calls=%async_computation | async-start | bytes 3145728 | tf_op jit(solution)/shard_map/all_to_all | solution.py:78
  62.2 41.1 %all-to-all-start.2 = ((bf16[16,48,1024]{2,1,0:T(8,128)(2,1)}), bf16[16,48,1024]{2,1,0:T(8,128)(2,1)S(1)}, u32[]{:S(2)}, u32[]{:S(2)}) async-start(bf16[16,48,1024]{2,1,0:T(8,128)(2,1)} %bitcast.63), calls=%async_computation.2 | async-start | bytes 3145728 | tf_op jit(solution)/shard_map/all_to_all | solution.py:88
  71.0 98.0 %reduce-scatter.5.cloned.1.call-start = ((), (), s32[]{:S(2)}) async-start(), calls=%async_computation.7 | async-start | bytes 1572864 | tf_op jit(solution)/shard_map/reduce_scatter | solution.py:121
  71.2 4.0 %copy-start.2 = (bf16[1,1024,512]{2,1,0:T(8,128)(2,1)S(1)}, bf16[1,1024,512]{2,1,0:T(8,128)(2,1)}, u32[]{:S(2)}) copy-start(bf16[1,1024,512]{2,1,0:T(8,128)(2,1)} %param.11) | copy-start | bytes 3145732
  103.3 4.4 %copy-start.4 = (bf16[1,1024,512]{2,1,0:T(8,128)(2,1)S(1)}, bf16[1,1024,512]{2,1,0:T(8,128)(2,1)}, u32[]{:S(2)}) copy-start(bf16[1,1024,512]{2,1,0:T(8,128)(2,1)} %param.10) | copy-start | bytes 3145732
  107.7 2.7 %copy-start.7 = (bf16[768,512]{0,1:T(8,128)(2,1)}, bf16[768,512]{0,1:T(8,128)(2,1)S(1)}, u32[]{:S(2)}) copy-start(bf16[768,512]{0,1:T(8,128)(2,1)S(1)} %get-tuple-element.17) | copy-start | bytes 2359300
  112.4 1.2 copy-start.3
  118.0 41.1 %all-to-all-start.3 = ((bf16[16,48,1024]{2,1,0:T(8,128)(2,1)}), bf16[16,48,1024]{2,1,0:T(8,128)(2,1)S(1)}, u32[]{:S(2)}, u32[]{:S(2)}) async-start(bf16[16,48,1024]{2,1,0:T(8,128)(2,1)} %bitcast.65), calls=%async_computation.3 | async-start | bytes 3145728 | tf_op jit(solution)/shard_map/all_to_all | solution.py:93
  126.8 88.0 %reduce-scatter.3.cloned.1.call-start = ((), (), s32[]{:S(2)}) async-start(), calls=%async_computation.6 | async-start | bytes 3145728 | tf_op jit(solution)/shard_map/reduce_scatter | solution.py:112
  131.6 1.1 copy-start.8
  159.1 1.1 copy-start.1
  160.2 41.2 %all-to-all-start.1 = ((bf16[16,48,1024]{2,1,0:T(8,128)(2,1)}), bf16[16,48,1024]{2,1,0:T(8,128)(2,1)}, u32[]{:S(2)}, u32[]{:S(2)}) async-start(bf16[16,48,1024]{2,1,0:T(8,128)(2,1)} %bitcast.66), calls=%async_computation.1 | async-start | bytes 3145728 | tf_op jit(solution)/shard_map/all_to_all | solution.py:81
Sparse Core Ops, SparseCore 0:
  112.6 23.7 reduce-scatter.4
  138.7 31.8 reduce-scatter.2
where the time goes:
time: 229 us; the launch traced here: 225 us
  waiting for transfers between devices  82.3 us (36%)
  local copies, waits for them, and re-layouts  44.3 us (19%)
  starting transfers between devices  34 us (15%)
  matrix products  28 us (12%)
  other arithmetic  21.8 us (10%)
  between operations  14.2 us (6%)
    all_to_all x1, waiting for transfers between devices, shards(): lax.all_to_all(send_grads, 'expert', split_axis=0, concat_axis=0, tiled=T...  24.5 us
    all_to_all x1, waiting for transfers between devices, shards(): lax.all_to_all(input_grads.reshape(experts, capacity, latent_width), 'exp...  24.2 us
    all_to_all x1, waiting for transfers between devices, shards(): lax.all_to_all(outputs.reshape(experts, capacity, latent_width), 'expert'...  20.1 us
    all_to_all x1, waiting for transfers between devices, shards(): lax.all_to_all(send_tokens, 'expert', split_axis=0, concat_axis=0, tiled=...  13.4 us
    scatter x1, other arithmetic, pack_rows(): buffer = buffer.at[slot_index].set(row_values)  10.1 us
    all_to_all x1, starting transfers between devices, shards(): lax.all_to_all(input_grads.reshape(experts, capacity, latent_width), 'exp...  8.76 us
    all_to_all x1, starting transfers between devices, shards(): lax.all_to_all(send_grads, 'expert', split_axis=0, concat_axis=0, tiled=T...  8.75 us
    all_to_all x1, starting transfers between devices, shards(): lax.all_to_all(outputs.reshape(experts, capacity, latent_width), 'expert'...  8.75 us
  transfers between devices with their start and end apart: 6, of which 4 were waited for; matrix products, arithmetic and copies ran while one was open for 28% of the time, Pallas kernels for 0%

commit v1 on v0

v1 whole, which is shorter than its diff:
```python
import jax
import jax.numpy as jnp
from jax import lax
from jax.sharding import PartitionSpec as P


def slot_selector(routes, route_weights, expert, capacity):
    named = routes == expert
    mask = jnp.any(named, axis=2)
    weight = jnp.sum(jnp.where(named, route_weights, 0.0), axis=2)
    counts = mask.astype(jnp.int32)
    rank = jnp.cumsum(counts, axis=1) - counts
    rank = jnp.where(mask, rank, capacity)
    select = rank[:, None, :] == jnp.arange(capacity, dtype=jnp.int32)[None, :, None]
    return select, weight


def shards(tokens, routes, route_weights, gate_weight, up_weight, down_weight, cotangent):
    rows, latent = tokens.shape
    top = routes.shape[1]
    experts = lax.axis_size("expert")
    capacity = rows * top // experts
    me = lax.axis_index("expert")
    gather = lambda v: lax.all_gather(v, "expert", axis=0, tiled=False)
    all_routes = gather(routes)
    all_weights = gather(route_weights)
    all_tokens = gather(tokens)
    all_cots = gather(cotangent)
    gate, up, down = gate_weight[0], up_weight[0], down_weight[0]
    select, weight = slot_selector(all_routes, all_weights, me, capacity)
    sel16 = select.astype(jnp.bfloat16)
    slot_weight = jnp.sum(jnp.where(select, weight[:, None, :], 0.0), axis=2)
    pick = (((2,), (1,)), ((0,), (0,)))
    inputs = lax.dot_general(sel16, all_tokens, pick, preferred_element_type=jnp.float32)
    inputs = inputs.astype(jnp.bfloat16).reshape(-1, latent)
    cot_rows = lax.dot_general(sel16, all_cots, pick, preferred_element_type=jnp.float32)
    out_grads = (cot_rows * slot_weight[:, :, None]).astype(jnp.bfloat16).reshape(-1, latent)

    dot = lambda a, b, d: lax.dot_general(a, b, (d, ((), ())), preferred_element_type=jnp.float32)
    gate_pre = dot(inputs, gate, ((1,), (0,)))
    up_pre = dot(inputs, up, ((1,), (0,)))
    sig = jax.nn.sigmoid(gate_pre)
    hidden = (gate_pre * sig * up_pre).astype(jnp.bfloat16)
    outputs = dot(hidden, down, ((1,), (0,))).astype(jnp.bfloat16)
    hidden_grad = dot(out_grads, down, ((1,), (1,)))
    up_gp = (hidden_grad * gate_pre * sig).astype(jnp.bfloat16)
    gate_gp = (hidden_grad * up_pre * sig * (1.0 + gate_pre * (1.0 - sig))).astype(jnp.bfloat16)
    slot_grad = (dot(gate_gp, gate, ((1,), (1,))) + dot(up_gp, up, ((1,), (1,)))).astype(jnp.bfloat16)

    put = (((1,), (1,)), ((0,), (0,)))
    out_part = lax.dot_general(
        sel16, outputs.reshape(experts, capacity, latent), put, preferred_element_type=jnp.float32
    )
    out_part = (out_part * weight[:, :, None]).astype(jnp.bfloat16)
    grad_part = lax.dot_general(
        sel16, slot_grad.reshape(experts, capacity, latent), put, preferred_element_type=jnp.float32
    ).astype(jnp.bfloat16)
    scatter = lambda v, axis, dim: lax.psum_scatter(v, axis, scatter_dimension=dim, tiled=True)
    mixed = scatter(out_part.reshape(-1, latent), "expert", 0)
    lgrad = scatter(grad_part.reshape(-1, latent), "expert", 0)

    pair = dot(inputs, jnp.concatenate([gate_gp, up_gp], axis=1), ((0,), (0,)))
    pair_share = scatter(pair.astype(jnp.bfloat16), "dp", 0).astype(jnp.float32)
    down_part = dot(out_grads, hidden, ((0,), (0,))).astype(jnp.bfloat16)
    down_share = scatter(down_part, "dp", 0).astype(jnp.float32)
    ffn = hidden.shape[1]
    return (mixed, lgrad, pair_share[:, :ffn][None], pair_share[:, ffn:][None], down_share.T[None])


def solution(mesh):
    rows = P(("dp", "expert"), None)
    per_expert = P("expert", None, None)
    return jax.shard_map(
        shards,
        mesh=mesh,
        in_specs=(rows, rows, rows, per_expert, per_expert, per_expert, rows),
        out_specs=(rows, rows, P("expert", "dp", None), P("expert", "dp", None), P("expert", None, "dp")),
        check_vma=False,
    )
```

time: 229 us -> 337 us (1.47)
  waiting for transfers between devices: 82.3 us -> 239 us
  blocking collectives: 0 us -> 41.8 us
  local copies, waits for them, and re-layouts: 44.3 us -> 4.89 us
  starting transfers between devices: 34 us -> 0.42 us
  other arithmetic: 21.8 us -> 3.19 us
    reduce_scatter x2 -> x4, waiting for transfers between devices: 0.02 us -> 181 us  [shards(): lax.psum_scatter(v, axis, scatter_dimension=dim, tiled=True)]
    all_to_all x4 -> x0, waiting for transfers between devices: 82.2 us -> none  [the longest x1 24.5 us: shards(): lax.all_to_all(send_grads, 'expert', split_axis=0, concat_axis=0, tiled=T...]
    all_gather x0 -> x2, waiting for transfers between devices: none -> 56.3 us  [shards(): gather = lambda v: lax.all_gather(v, 'expert', axis=0, tiled=False)]
    all_gather x0 -> x2, blocking collectives: none -> 41.8 us  [shards(): gather = lambda v: lax.all_gather(v, 'expert', axis=0, tiled=False)]
    all_to_all x4 -> x0, starting transfers between devices: 33.7 us -> none  [the longest x1 8.76 us: shards(): lax.all_to_all(input_grads.reshape(experts, capacity, latent_width), 'exp...]
    scatter x1 -> x0, other arithmetic: 10.1 us -> none  [pack_rows(): buffer = buffer.at[slot_index].set(row_values)]
    mul x5 -> x0, local copies, waits for them, and re-layouts: 7.61 us -> none  [the longest x2 7.22 us: shards(): kept_weights[:, :, None] * cotangent[:, None, :].astype(jnp.float32)]
    gather x2 -> x0, local copies, waits for them, and re-layouts: 7.13 us -> none  [unpack_rows(): return padded[slot_index].reshape(-1, top_count, latent_width)]
  transfers between devices with their start and end apart: 6 -> 6, of which waited for: 4 -> 6; matrix products, arithmetic and copies ran while one was open for 28% -> 9% of each run, Pallas kernels for 0% -> 0%
where the time goes in v1:
time: 337 us; the launch traced here: 334 us
  waiting for transfers between devices  239 us (71%)
  blocking collectives  41.8 us (12%)
  matrix products  30.3 us (9%)
  between operations  14.3 us (4%)
  local copies, waits for them, and re-layouts  4.89 us (1%)
    reduce_scatter x4, waiting for transfers between devices, shards(): lax.psum_scatter(v, axis, scatter_dimension=dim, tiled=True)  181 us
    all_gather x2, waiting for transfers between devices, shards(): gather = lambda v: lax.all_gather(v, 'expert', axis=0, tiled=False)  56.3 us
    all_gather x2, blocking collectives, shards(): gather = lambda v: lax.all_gather(v, 'expert', axis=0, tiled=False)  41.8 us
    dot_general x8, matrix products, shards(): lax.dot_general(a, b, (d, ((), ())), preferred_element_type=jnp.float32)  17.7 us
  transfers between devices with their start and end apart: 6, of which 6 were waited for; matrix products, arithmetic and copies ran while one was open for 9% of the time, Pallas kernels for 0%

profile of v1, /device:TPU:1, one launch (start us, length us, event | category | flops | bytes accessed | tf_op | source)
XLA Modules:
  0.0 334.0 jit_solution(9489342486632225022)
XLA Ops:
  8.7 23.5 %all-gather = s32[2048,6]{0,1:T(8,128)S(1)} all-gather(s32[128,6]{0,1:T(8,128)} %param.8), channel_id=2, replica_groups=mesh['dp'=2,'expert'=16] {'expert'}, dimensions={0}, use_global_device_ids=true | all-gather | bytes 52224 | tf_op jit(solution)/shard_map/all_gather | solution.py:24
  32.5 18.3 %all-gather.2 = f32[2048,6]{0,1:T(8,128)S(1)} all-gather(f32[128,6]{0,1:T(8,128)} %param.9), channel_id=4, replica_groups=mesh['dp'=2,'expert'=16] {'expert'}, dimensions={0}, use_global_device_ids=true | all-gather | bytes 52224 | tf_op jit(solution)/shard_map/all_gather | solution.py:24
  51.1 12.4 %all-gather.7.cloned.1.call-done = bf16[2048,1024]{1,0:T(8,128)(2,1)} async-done(((bf16[128,1024]{1,0:T(8,128)(2,1)}), bf16[2048,1024]{1,0:T(8,128)(2,1)}) %all-gather.7.cloned.1.call-update) | async-done | bytes 4194320 | tf_op jit(solution)/shard_map/all_gather | solution.py:24
  63.5 3.0 convolution_convert_fusion.3
  66.5 2.2 fusion.11
  68.7 2.2 fusion.7
  70.9 43.9 %all-gather.9.cloned.1.call-done = bf16[2048,1024]{1,0:T(8,128)(2,1)} async-done(((bf16[128,1024]{1,0:T(8,128)(2,1)}), bf16[2048,1024]{1,0:T(8,128)(2,1)}) %all-gather.9.cloned.1.call-update) | async-done | bytes 4194320 | tf_op jit(solution)/shard_map/all_gather | solution.py:24
  114.9 3.0 multiply_convert_fusion.1
  118.0 2.5 multiply_convert_fusion.2
  121.4 2.0 convolution_convert_fusion.4
  123.5 4.3 %convolution_convert_fusion.1 = bf16[1024,1024]{1,0:T(8,128)(2,1)} fusion(bf16[768,1024]{1,0:T(8,128)(2,1)S(1)} %bitcast.59, bf16[768,512]{0,1:T(8,128)(2,1)} %get-tuple-element.12, bf16[768,512]{0,1:T(8,128)(2,1)S(1)} %get-tuple-element.13), kind=kOutput, calls=%fused_computation.4 | convolution fusion | flops 1614807040 | bytes 5242880 | tf_op jit(solution)/shard_map/dot_general | solution.py:39
  128.1 2.4 fusion.9
  130.5 1.1 add_convert_fusion
  131.5 3.3 convolution_convert_fusion
  134.9 1.1 copy-done.8
  137.0 3.3 multiply_convert_fusion
  140.3 1.7 reduce-scatter.11.cloned.1.call-done
  141.9 1.2 convert_bitcast_fusion
  143.1 1.3 copy.12
  144.4 31.6 %reduce-scatter.9.cloned.1.call-done = bf16[512,1024]{1,0:T(8,128)(2,1)} async-done(((bf16[1024,1024]{1,0:T(8,128)(2,1)}), bf16[512,1024]{1,0:T(8,128)(2,1)}) %reduce-scatter.9.cloned.1.call-update) | async-done | bytes 1048592 | tf_op jit(solution)/shard_map/reduce_scatter | solution.py:58
  176.0 1.5 convert_element_type.60
  177.5 1.5 slice_bitcast_fusion
  179.0 71.9 %reduce-scatter.7.cloned.1.call-done = bf16[128,1024]{1,0:T(8,128)(2,1)} async-done(((bf16[2048,1024]{1,0:T(8,128)(2,1)}), bf16[128,1024]{1,0:T(8,128)(2,1)}) %reduce-scatter.7.cloned.1.call-update) | async-done | bytes 262160 | tf_op jit(solution)/shard_map/reduce_scatter | solution.py:58
  250.9 76.3 %reduce-scatter.5.cloned.1.call-done = bf16[128,1024]{1,0:T(8,128)(2,1)} async-done(((bf16[2048,1024]{1,0:T(8,128)(2,1)}), bf16[128,1024]{1,0:T(8,128)(2,1)}) %reduce-scatter.5.cloned.1.call-update) | async-done | bytes 262160 | tf_op jit(solution)/shard_map/reduce_scatter | solution.py:58
  (36 shorter events, 4.4 us)
Async XLA Ops:
  7.2 110.7 %copy-start = (bf16[1,512,1024]{2,1,0:T(8,128)(2,1)S(1)}, bf16[1,512,1024]{2,1,0:T(8,128)(2,1)}, u32[]{:S(2)}) copy-start(bf16[1,512,1024]{2,1,0:T(8,128)(2,1)} %param.12) | copy-start | bytes 3145732
  7.2 56.3 %all-gather.7.cloned.1.call-start = ((), (), s32[]{:S(2)}) async-start(), calls=%async_computation.8 | async-start | bytes 4456448 | tf_op jit(solution)/shard_map/all_gather | solution.py:24
  7.9 106.9 %all-gather.9.cloned.1.call-start = ((), (), s32[]{:S(2)}) async-start(), calls=%async_computation.9 | async-start | bytes 4456448 | tf_op jit(solution)/shard_map/all_gather | solution.py:24
  8.7 133.3 %reduce-scatter.11.cloned.1.call-start = ((), (), s32[]{:S(2)}) async-start(), calls=%async_computation.7 | async-start | bytes 1572864 | tf_op jit(solution)/shard_map/reduce_scatter | solution.py:58
  63.5 3.0 copy-start.3
  66.5 2.2 copy-start.1
  114.9 3.0 copy-start.5
  114.9 3.1 copy-start.6
  120.5 0.9 copy-start.7
  123.4 52.6 %reduce-scatter.9.cloned.1.call-start = ((), (), s32[]{:S(2)}) async-start(), calls=%async_computation.6 | async-start | bytes 3145728 | tf_op jit(solution)/shard_map/reduce_scatter | solution.py:58
  127.8 2.7 copy-start.2
  127.8 123.1 %reduce-scatter.7.cloned.1.call-start = ((), (), s32[]{:S(2)}) async-start(), calls=%async_computation.5 | async-start | bytes 4456448 | tf_op jit(solution)/shard_map/reduce_scatter | solution.py:58
  128.1 2.4 copy-start.4
  134.8 1.1 copy-start.8
  134.8 192.4 %reduce-scatter.5.cloned.1.call-start = ((), (), s32[]{:S(2)}) async-start(), calls=%async_computation.4 | async-start | bytes 4456448 | tf_op jit(solution)/shard_map/reduce_scatter | solution.py:58
Sparse Core Ops, SparseCore 0:
  10.2 53.2 all-gather.6
  65.7 49.1 all-gather.8
  123.5 18.3 reduce-scatter.10
  144.1 31.8 reduce-scatter.8
  180.3 70.6 reduce-scatter.6
  255.7 71.4 reduce-scatter.4

commit v2 on v1

v2 whole, which is shorter than its diff:
```python
import functools
import math

import jax
import jax.numpy as jnp
from jax import lax
from jax.experimental import pallas as pl
from jax.experimental.pallas import tpu as pltpu
from jax.sharding import PartitionSpec as P

F32, BF16 = jnp.float32, jnp.bfloat16


def dot(a, b, contract):
    return lax.dot_general(a, b, (contract, ((), ())), preferred_element_type=F32)


ROWS_COLS = ((1,), (0,))
LAST_LAST = ((1,), (1,))
FIRST_FIRST = ((0,), (0,))


def kernel(
    side, nd, capacity, cap,
    routes_ref, weights_ref, tok_ref, cot_ref, gate_ref, up_ref, down_ref,
    mixed_ref, lgrad_ref, gate_out, up_out, down_out,
    meta, line, stage, inbox, back_stage, back, part, hop, gate_pre, up_pre, hid, gate_gp, up_gp,
    dp_gate, dp_up, dp_down, in_gate, in_up, in_down,
    meta_send, meta_recv, line_send, line_recv, slot_send, slot_recv, back_send, back_recv,
    hop_send, hop_recv, dp_send, dp_recv,
):
    experts = side * side
    top, rows = routes_ref.shape
    latent = tok_ref.shape[1]
    ffn = gate_ref.shape[1]
    share = latent // nd
    slots = side * cap
    me = lax.axis_index("expert")
    dp = lax.axis_index("dp")
    z, p = me // side, me % side

    def at_line(k):
        return {"expert": k * side + p}

    def at_plane(k):
        return {"expert": z * side + k}

    def remote(src, dst, send, recv, device):
        return pltpu.make_async_remote_copy(
            src_ref=src, dst_ref=dst, send_sem=send, recv_sem=recv,
            device_id=device, device_id_type=pl.DeviceIdType.MESH,
        )

    def others(count, mine, body):
        def turn(r, carry):
            body((mine + r) % count)
            return carry
        lax.fori_loop(1, count, turn, 0)

    def loop(count, body):
        def turn(i, carry):
            body(i)
            return carry
        lax.fori_loop(0, count, turn, 0)

    barrier = pltpu.get_barrier_semaphore()

    def greet(device):
        pl.semaphore_signal(barrier, inc=1, device_id=device, device_id_type=pl.DeviceIdType.MESH)

    others(side, z, lambda k: greet(at_line(k)))
    others(side, p, lambda k: greet(at_plane(k)))
    others(nd, dp, lambda k: greet({"dp": k}))

    name = lax.broadcasted_iota(jnp.int32, (experts, rows), 0)
    mask = jnp.zeros((experts, rows), F32)
    weight = jnp.zeros((experts, rows), F32)
    for k in range(top):
        named = routes_ref[k : k + 1, :] == name
        mask = jnp.where(named, 1.0, mask)
        weight = jnp.where(named, weights_ref[k : k + 1, :], weight)
    before = lax.broadcasted_iota(jnp.int32, (rows, rows), 0) < lax.broadcasted_iota(
        jnp.int32, (rows, rows), 1
    )
    rank = dot(mask.astype(BF16), jnp.where(before, 1.0, 0.0).astype(BF16), ROWS_COLS)
    kept = jnp.where(rank < float(capacity), mask, 0.0)
    meta[z, 0:experts, :] = jnp.where(kept > 0.0, rank, -1.0)
    meta[z, experts : 2 * experts, :] = weight
    line[0, z] = tok_ref[...]
    line[1, z] = cot_ref[...]

    pl.semaphore_wait(barrier, 2 * (side - 1) + nd - 1)

    def meta_copy(src, dst):
        return remote(meta.at[src], meta.at[src], meta_send.at[dst], meta_recv.at[src], at_line(dst))

    def line_copy(t, way, block, dst):
        return remote(
            line.at[t, block], line.at[t, block], line_send.at[t, way, block],
            line_recv.at[t, block], at_line(dst),
        )

    def rows_of(block):
        return pl.ds(pl.multiple_of(block * cap, cap), cap)

    def slot_copy(t, src, dst, block):
        return remote(
            stage.at[t, dst, rows_of(block)], inbox.at[t, src, rows_of(block)],
            slot_send.at[t, dst, block], slot_recv.at[t, src, block], at_plane(dst),
        )

    def back_copy(t, src, dst):
        return remote(
            back_stage.at[t, dst], back.at[t, src], back_send.at[t, dst], back_recv.at[t, src],
            at_plane(dst),
        )

    def hop_copy(t, way, block, dst):
        return remote(
            part.at[t, block], hop.at[t, way, block], hop_send.at[t, way, block],
            hop_recv.at[t, way, block], at_line(dst),
        )

    def dp_copy(kind, src, dst):
        out, come = ((dp_gate, in_gate), (dp_up, in_up), (dp_down, in_down))[kind]
        return remote(
            out.at[dst], come.at[src], dp_send.at[kind, dst], dp_recv.at[kind, src], {"dp": dst}
        )

    others(side, z, lambda k: meta_copy(z, k).start())

    slot_name = lax.broadcasted_iota(jnp.int32, (cap, rows), 0).astype(F32)

    def selector(block):
        hot, scaled = [], []
        for q in range(side):
            ranks = meta[block, pl.ds(z * side + q, 1), :]
            scale = meta[block, pl.ds(experts + z * side + q, 1), :]
            hit = slot_name == ranks
            hot.append(jnp.where(hit, 1.0, 0.0))
            scaled.append(jnp.where(hit, scale, 0.0))
        return jnp.concatenate(hot, axis=0), jnp.concatenate(scaled, axis=0)

    def pack(t, block):
        hot, scaled = selector(block)
        picked = dot(hot.astype(BF16), line[t, block], ROWS_COLS)
        if t == 1:
            picked = picked * jnp.sum(scaled, axis=1, keepdims=True)
        picked = picked.astype(BF16)
        for q in range(side):
            stage[t, q, rows_of(block), :] = picked[q * cap : (q + 1) * cap]
        others(side, p, lambda q: slot_copy(t, p, q, block).start())
        inbox[t, p, rows_of(block), :] = stage[t, p, rows_of(block), :]

    def arrive(t, d):
        def come(block):
            @pl.when(d > 0)
            def _():
                if t == 0:
                    meta_copy(block, z).wait_recv()
                line_copy(t, 0, block, z).wait_recv()

        @pl.when(z - d >= 0)
        def _():
            come(z - d)

            @pl.when(z + 1 < side)
            def _():
                line_copy(t, 0, z - d, z + 1).start()

        @pl.when(z + d < side)
        def _():
            come(z + d)

            @pl.when(z > 0)
            def _():
                line_copy(t, 1, z + d, z - 1).start()

        @pl.when(z - d >= 0)
        def _():
            pack(t, z - d)

        @pl.when((d > 0) & (z + d < side))
        def _():
            pack(t, z + d)

    def slots_in(t, src):
        @pl.when(src != p)
        def _():
            loop(side, lambda block: slot_copy(t, src, p, block).wait_recv())

    def hand_back(t, dst, value):
        back_stage[t, dst] = value

        @pl.when(dst != p)
        def _():
            back_copy(t, p, dst).start()

        @pl.when(dst == p)
        def _():
            back[t, p] = back_stage[t, p]

    def forward(src):
        slots_in(0, src)
        inputs = inbox[0, src]
        pre = dot(inputs, gate_ref[...], ROWS_COLS)
        raised = dot(inputs, up_ref[...], ROWS_COLS)
        gate_pre[src] = pre
        up_pre[src] = raised
        hidden = (pre * jax.nn.sigmoid(pre) * raised).astype(BF16)
        hid[src] = hidden
        hand_back(0, src, dot(hidden, down_ref[...], ROWS_COLS).astype(BF16))

    def backward(src):
        pre, raised = gate_pre[src], up_pre[src]
        sig = jax.nn.sigmoid(pre)
        hidden_grad = dot(inbox[1, src], down_ref[...], LAST_LAST)
        up_g = (hidden_grad * pre * sig).astype(BF16)
        gate_g = (hidden_grad * raised * sig * (1.0 + pre * (1.0 - sig))).astype(BF16)
        up_gp[src] = up_g
        gate_gp[src] = gate_g
        slot_grad = dot(gate_g, gate_ref[...], LAST_LAST) + dot(up_g, up_ref[...], LAST_LAST)
        hand_back(1, src, slot_grad.astype(BF16))

    loop(side, lambda d: arrive(0, d))

    def cot_and_forward(d):
        arrive(1, d)
        forward((p + d) % side)

    loop(side, cot_and_forward)

    def columns(j):
        return pl.ds(pl.multiple_of(j * share, share), share)

    def flat(ref, width):
        return ref.reshape(side * slots, width)

    def weight_part(kind, j):
        if kind == 2:
            grads = flat(inbox[1, :, :, columns(j)], share)
            return dot(flat(hid[...], ffn), grads, FIRST_FIRST).astype(BF16)
        grads = flat((gate_gp if kind == 0 else up_gp)[...], ffn)
        return dot(flat(inbox[0, :, :, columns(j)], share), grads, FIRST_FIRST).astype(BF16)

    def share_out(kind):
        def one(j):
            (dp_gate, dp_up, dp_down)[kind][j] = weight_part(kind, j)
            dp_copy(kind, dp, j).start()
        others(nd, dp, one)

    others(side, p, lambda src: slots_in(1, src))
    share_out(2)
    loop(side, lambda r: backward((p + r) % side))
    share_out(0)
    share_out(1)

    def combine(t, block):
        hot, scaled = selector(block)
        values = back[t, :, rows_of(block), :].reshape(side * cap, latent)
        if t == 1:
            return dot(hot.astype(BF16), values, FIRST_FIRST)
        high = scaled.astype(BF16)
        low = (scaled - high.astype(F32)).astype(BF16)
        return dot(high, values, FIRST_FIRST) + dot(low, values, FIRST_FIRST)

    def pass_on(t, way, block, dst, has_prior):
        total = combine(t, block)
        part[t, block] = total.astype(BF16)

        @pl.when(has_prior)
        def _():
            hop_copy(t, way, block, z).wait_recv()
            part[t, block] = (part[t, block].astype(F32) + hop[t, way, block].astype(F32)).astype(BF16)

        hop_copy(t, way, block, dst).start()

    def reduce_line(t):
        others(side, p, lambda src: back_copy(t, src, p).wait_recv())

        def step(i):
            @pl.when(side - 1 - i > z)
            def _():
                pass_on(t, 0, side - 1 - i, z + 1, z > 0)

            @pl.when(i < z)
            def _():
                pass_on(t, 1, i, z - 1, z + 1 < side)

        loop(side - 1, step)

    def finish(t, out):
        out[...] = combine(t, z).astype(BF16)

        def add(way):
            hop_copy(t, way, z, z).wait_recv()
            out[...] = (out[...].astype(F32) + hop[t, way, z].astype(F32)).astype(BF16)

        @pl.when(z > 0)
        def _():
            add(0)

        @pl.when(z + 1 < side)
        def _():
            add(1)

    reduce_line(0)
    reduce_line(1)
    finish(0, mixed_ref)
    for kind, out in ((2, down_out), (0, gate_out), (1, up_out)):
        out[0] = weight_part(kind, dp).astype(F32)
    finish(1, lgrad_ref)
    for kind, out, come in ((2, down_out, in_down), (0, gate_out, in_gate), (1, up_out, in_up)):
        def add_share(j):
            dp_copy(kind, j, dp).wait_recv()
            out[0] = out[0] + come[j].astype(F32)
        others(nd, dp, add_share)

    others(side, z, lambda k: meta_copy(z, k).wait_send())
    for t in range(2):
        def line_sent(block):
            @pl.when((block <= z) & (z + 1 < side))
            def _():
                line_copy(t, 0, block, z + 1).wait_send()

            @pl.when((block >= z) & (z > 0))
            def _():
                line_copy(t, 1, block, z - 1).wait_send()

            @pl.when(block > z)
            def _():
                hop_copy(t, 0, block, z + 1).wait_send()

            @pl.when(block < z)
            def _():
                hop_copy(t, 1, block, z - 1).wait_send()

        loop(side, line_sent)

        def plane_sent(q):
            loop(side, lambda block: slot_copy(t, p, q, block).wait_send())
            back_copy(t, p, q).wait_send()

        others(side, p, plane_sent)
    for kind in range(3):
        others(nd, dp, lambda j: dp_copy(kind, dp, j).wait_send())


def shards(tokens, routes, route_weights, gate_weight, up_weight, down_weight, cotangent):
    rows, latent = tokens.shape
    top = routes.shape[1]
    ffn = gate_weight.shape[2]
    experts, nd = lax.axis_size("expert"), lax.axis_size("dp")
    side = math.isqrt(experts)
    assert side * side == experts
    capacity = rows * top // experts
    cap = -(-capacity // 16) * 16
    slots, share = side * cap, latent // nd
    vmem = pl.BlockSpec(memory_space=pltpu.VMEM)
    dma = lambda *shape: pltpu.SemaphoreType.DMA(shape)
    return pl.pallas_call(
        functools.partial(kernel, side, nd, capacity, cap),
        out_shape=(
            jax.ShapeDtypeStruct((rows, latent), BF16),
            jax.ShapeDtypeStruct((rows, latent), BF16),
            jax.ShapeDtypeStruct((1, share, ffn), F32),
            jax.ShapeDtypeStruct((1, share, ffn), F32),
            jax.ShapeDtypeStruct((1, ffn, share), F32),
        ),
        in_specs=[vmem] * 7,
        out_specs=[vmem] * 5,
        scratch_shapes=[
            pltpu.VMEM((side, 2 * experts, rows), F32),
            pltpu.VMEM((2, side, rows, latent), BF16),
            pltpu.VMEM((2, side, slots, latent), BF16),
            pltpu.VMEM((2, side, slots, latent), BF16),
            pltpu.VMEM((2, side, slots, latent), BF16),
            pltpu.VMEM((2, side, slots, latent), BF16),
            pltpu.VMEM((2, side, rows, latent), BF16),
            pltpu.VMEM((2, 2, side, rows, latent), BF16),
            pltpu.VMEM((side, slots, ffn), F32),
            pltpu.VMEM((side, slots, ffn), F32),
            pltpu.VMEM((side, slots, ffn), BF16),
            pltpu.VMEM((side, slots, ffn), BF16),
            pltpu.VMEM((side, slots, ffn), BF16),
            pltpu.VMEM((nd, share, ffn), BF16),
            pltpu.VMEM((nd, share, ffn), BF16),
            pltpu.VMEM((nd, ffn, share), BF16),
            pltpu.VMEM((nd, share, ffn), BF16),
            pltpu.VMEM((nd, share, ffn), BF16),
            pltpu.VMEM((nd, ffn, share), BF16),
            dma(side), dma(side),
            dma(2, 2, side), dma(2, side),
            dma(2, side, side), dma(2, side, side),
            dma(2, side), dma(2, side),
            dma(2, 2, side), dma(2, 2, side),
            dma(3, nd), dma(3, nd),
        ],
        compiler_params=pltpu.CompilerParams(
            collective_id=0, has_side_effects=True, vmem_limit_bytes=60 * 1024 * 1024
        ),
    )(
        routes.T, route_weights.T, tokens, cotangent, gate_weight[0], up_weight[0], down_weight[0]
    )


def solution(mesh):
    rows = P(("dp", "expert"), None)
    per_expert = P("expert", None, None)
    return jax.shard_map(
        shards,
        mesh=mesh,
        in_specs=(rows, rows, rows, per_expert, per_expert, per_expert, rows),
        out_specs=(
            rows, rows, P("expert", "dp", None), P("expert", "dp", None), P("expert", None, "dp")
        ),
        check_vma=False,
    )
```

time: 337 us -> 129 us (0.38)
  waiting for transfers between devices: 239 us -> 0 us
  Pallas kernels: 0 us -> 120 us
  blocking collectives: 41.8 us -> 0 us
  matrix products: 30.3 us -> 0 us
  between operations: 14.3 us -> 0.65 us
    reduce_scatter x4 -> x0, waiting for transfers between devices: 181 us -> none  [shards(): lax.psum_scatter(v, axis, scatter_dimension=dim, tiled=True)]
    pallas_call x0 -> x1, Pallas kernels: none -> 120 us  [shards(): pl.pallas_call(functools.partial(kernel, side, nd, capacity, cap), out_sh...]
    all_gather x2 -> x0, waiting for transfers between devices: 56.3 us -> none  [shards(): gather = lambda v: lax.all_gather(v, 'expert', axis=0, tiled=False)]
    all_gather x2 -> x0, blocking collectives: 41.8 us -> none  [shards(): gather = lambda v: lax.all_gather(v, 'expert', axis=0, tiled=False)]
    dot_general x12 -> x0, matrix products: 30.3 us -> none  [the longest x8 17.7 us: shards(): lax.dot_general(a, b, (d, ((), ())), preferred_element_type=jnp.float32)]
    unnamed x19 -> x11, local copies, waits for them, and re-layouts: 3.38 us -> 7.6 us
  transfers between devices with their start and end apart: 6 -> 0, of which waited for: 6 -> 0; matrix products, arithmetic and copies ran while one was open for 9% -> 0% of each run, Pallas kernels for 0% -> 0%
where the time goes in v2:
time: 129 us; the launch traced here: 128 us
  Pallas kernels  120 us (93%)
  local copies, waits for them, and re-layouts  7.6 us (6%)
    pallas_call x1, Pallas kernels, shards(): pl.pallas_call(functools.partial(kernel, side, nd, capacity, cap), out_sh...  120 us
    unnamed x11, local copies, waits for them, and re-layouts  7.6 us

profile of v2, /device:TPU:1, one launch (start us, length us, event | category | flops | bytes accessed | tf_op | source)
XLA Modules:
  0.0 128.4 jit_solution(16342242634281811351)
XLA Ops:
  0.6 120.2 %shard_map.110 = (bf16[128,1024]{1,0:T(8,128)(2,1)}, bf16[128,1024]{1,0:T(8,128)(2,1)}, f32[1,512,512]{2,1,0:T(8,128)}, f32[1,512,512]{2,1,0:T(8,128)}, f32[1,512,512]{2,1,0:T(8,128)}) custom-call(s32[6,128]{1,0:T(8,128)} %bitcast.8, f32[6,128]{1,0:T(8,128)} %bitcast.9, bf16[128,1024]{1,0:T(8,128)(2,1)} %tok_ref.1, bf16[128,1024]{1,0:T(8,128)(2,1)} %cot_ref.1, ...), custom_call_target="tpu_custom_call" | custom-call | tf_op jit(solution)/shard_map/pallas_call | solution.py:361
  120.8 0.0 copy-start.2
  120.8 1.8 %copy.17 = bf16[128,1024]{1,0:T(8,128)(2,1)} copy(bf16[128,1024]{1,0:T(8,128)(2,1)} %get-tuple-element.10) | data formatting | bytes 524288
  122.6 1.7 %copy.18 = bf16[128,1024]{1,0:T(8,128)(2,1)} copy(bf16[128,1024]{1,0:T(8,128)(2,1)} %get-tuple-element.11) | data formatting | bytes 524288
  124.2 0.0 copy-done.2
  124.2 0.0 copy-start.1
  124.2 1.0 copy.19
  125.2 0.6 copy-done.1
  125.8 0.0 copy-start
  125.8 1.0 copy.20
  126.8 0.6 copy-done
  127.4 1.0 copy.21
Async XLA Ops:
  120.8 3.4 %copy-start.2 = (f32[1,512,512]{2,1,0:T(8,128)S(1)}, f32[1,512,512]{2,1,0:T(8,128)}, u32[]{:S(2)}) copy-start(f32[1,512,512]{2,1,0:T(8,128)} %get-tuple-element.12) | copy-start | bytes 3145732
  124.2 1.6 %copy-start.1 = (f32[1,512,512]{2,1,0:T(8,128)S(1)}, f32[1,512,512]{2,1,0:T(8,128)}, u32[]{:S(2)}) copy-start(f32[1,512,512]{2,1,0:T(8,128)} %get-tuple-element.13) | copy-start | bytes 3145732
  125.8 1.6 %copy-start = (f32[1,512,512]{2,1,0:T(8,128)S(1)}, f32[1,512,512]{2,1,0:T(8,128)}, u32[]{:S(2)}) copy-start(f32[1,512,512]{2,1,0:T(8,128)} %get-tuple-element.14) | copy-start | bytes 3145732

commit v3 on v2

v3 whole, which is shorter than its diff:
```python
import functools
import math

import jax
import jax.numpy as jnp
from jax import lax
from jax.experimental import pallas as pl
from jax.experimental.pallas import tpu as pltpu
from jax.sharding import PartitionSpec as P

F32, BF16 = jnp.float32, jnp.bfloat16


def dot(a, b, contract):
    return lax.dot_general(a, b, (contract, ((), ())), preferred_element_type=F32)


ROWS_COLS = ((1,), (0,))
LAST_LAST = ((1,), (1,))
FIRST_FIRST = ((0,), (0,))


def kernel(
    side, nd, capacity, cap,
    routes_ref, weights_ref, tok_hbm, cot_hbm, gate_hbm, up_hbm, down_hbm,
    mixed_ref, lgrad_ref, gate_parts, up_parts, down_parts,
    gate_ref, up_ref, down_ref,
    meta, line, stage, inbox, back_stage, back, part, hop, gate_pre, up_pre, hid, gate_gp, up_gp,
    dp_gate, dp_up, dp_down,
    load_sem, meta_send, meta_recv, line_send, line_recv, slot_send, slot_recv, back_send,
    back_recv, hop_send, hop_recv, dp_send, dp_recv,
):
    experts = side * side
    top, rows = routes_ref.shape
    latent, ffn = gate_ref.shape
    share = latent // nd
    width = side * cap
    me = lax.axis_index("expert")
    dp = lax.axis_index("dp")
    z, p = me // side, me % side

    def at_line(k):
        return {"expert": k * side + p}

    def at_plane(k):
        return {"expert": z * side + k}

    def remote(src, dst, send, recv, device):
        return pltpu.make_async_remote_copy(
            src_ref=src, dst_ref=dst, send_sem=send, recv_sem=recv,
            device_id=device, device_id_type=pl.DeviceIdType.MESH,
        )

    def loop(first, last, body):
        def turn(i, carry):
            body(i)
            return carry
        lax.fori_loop(first, last, turn, 0)

    def others(count, mine, body):
        loop(1, count, lambda r: body((mine + r) % count))

    loads = [
        pltpu.make_async_copy(src, dst, load_sem.at[i])
        for i, (src, dst) in enumerate((
            (tok_hbm, line.at[0, z]), (cot_hbm, line.at[1, z]),
            (gate_hbm, gate_ref), (up_hbm, up_ref), (down_hbm, down_ref),
        ))
    ]
    for load in loads:
        load.start()

    barrier = pltpu.get_barrier_semaphore()

    def greet(device):
        pl.semaphore_signal(barrier, inc=1, device_id=device, device_id_type=pl.DeviceIdType.MESH)

    others(side, z, lambda k: greet(at_line(k)))
    others(side, p, lambda k: greet(at_plane(k)))
    others(nd, dp, lambda k: greet({"dp": k}))

    name = lax.broadcasted_iota(jnp.int32, (experts, rows), 0)
    mask = jnp.zeros((experts, rows), F32)
    weight = jnp.zeros((experts, rows), F32)
    for k in range(top):
        named = routes_ref[k : k + 1, :] == name
        mask = jnp.where(named, 1.0, mask)
        weight = jnp.where(named, weights_ref[k : k + 1, :], weight)
    before = lax.broadcasted_iota(jnp.int32, (rows, rows), 0) < lax.broadcasted_iota(
        jnp.int32, (rows, rows), 1
    )
    rank = dot(mask.astype(BF16), jnp.where(before, 1.0, 0.0).astype(BF16), ROWS_COLS)
    kept = jnp.where(rank < float(capacity), mask, 0.0)
    meta[z, 0:experts, :] = jnp.where(kept > 0.0, rank, -1.0)
    meta[z, experts : 2 * experts, :] = weight
    loads[0].wait()
    pl.semaphore_wait(barrier, 2 * (side - 1) + nd - 1)

    def meta_copy(src, dst):
        return remote(meta.at[src], meta.at[src], meta_send.at[dst], meta_recv.at[src], at_line(dst))

    def line_copy(t, way, block, dst):
        return remote(
            line.at[t, block], line.at[t, block], line_send.at[t, way, block],
            line_recv.at[t, block], at_line(dst),
        )

    def slot_copy(t, block, src, dst):
        return remote(
            stage.at[t, block, dst], inbox.at[t, block, src],
            slot_send.at[t, block, dst], slot_recv.at[t, block, src], at_plane(dst),
        )

    def back_copy(t, block, src, dst):
        return remote(
            back_stage.at[t, block, dst], back.at[t, block, src],
            back_send.at[t, block, dst], back_recv.at[t, block, src], at_plane(dst),
        )

    def hop_copy(t, way, block, dst):
        return remote(
            part.at[t, block], hop.at[t, way, block], hop_send.at[t, way, block],
            hop_recv.at[t, way, block], at_line(dst),
        )

    def dp_copy(kind, src, dst):
        out, come = ((dp_gate, gate_parts), (dp_up, up_parts), (dp_down, down_parts))[kind]
        return remote(
            out.at[dst], come.at[src], dp_send.at[kind, dst], dp_recv.at[kind, src], {"dp": dst}
        )

    def own_share(kind):
        out, come = ((dp_gate, gate_parts), (dp_up, up_parts), (dp_down, down_parts))[kind]
        return pltpu.make_async_copy(out.at[dp], come.at[dp], dp_send.at[kind, dp])

    slot_name = lax.broadcasted_iota(jnp.int32, (cap, rows), 0).astype(F32)

    def selector(block):
        hot, scaled = [], []
        for q in range(side):
            ranks = meta[block, pl.ds(z * side + q, 1), :]
            scale = meta[block, pl.ds(experts + z * side + q, 1), :]
            hit = slot_name == ranks
            hot.append(jnp.where(hit, 1.0, 0.0))
            scaled.append(jnp.where(hit, scale, 0.0))
        return jnp.concatenate(hot, axis=0), jnp.concatenate(scaled, axis=0)

    def visit(d, body):
        def one(s):
            block = z - d + 2 * d * s

            @pl.when((block >= 0) & (block < side) & (d + 1 > s))
            def _():
                body(block)
        loop(0, 2, one)

    def pack(t, block):
        hot, scaled = selector(block)
        picked = dot(hot.astype(BF16), line[t, block], ROWS_COLS)
        if t == 1:
            picked = picked * jnp.sum(scaled, axis=1, keepdims=True)
        stage[t, block] = picked.astype(BF16).reshape(side, cap, latent)
        others(side, p, lambda q: slot_copy(t, block, p, q).start())
        inbox[t, block, p] = stage[t, block, p]

    def arrive(t, d):
        def come(block):
            @pl.when(d > 0)
            def _():
                if t == 0:
                    meta_copy(block, z).wait_recv()
                line_copy(t, 0, block, z).wait_recv()

        @pl.when(z - d >= 0)
        def _():
            come(z - d)

            @pl.when(z + 1 < side)
            def _():
                line_copy(t, 0, z - d, z + 1).start()

        @pl.when(z + d < side)
        def _():
            come(z + d)

            @pl.when(z > 0)
            def _():
                line_copy(t, 1, z + d, z - 1).start()

        if t == 0:
            @pl.when(d == 0)
            def _():
                others(side, z, lambda k: meta_copy(z, k).start())
        visit(d, lambda block: pack(t, block))

    def hand_back(t, block, value):
        back_stage[t, block] = value.astype(BF16).reshape(side, cap, latent)
        others(side, p, lambda q: back_copy(t, block, p, q).start())
        back[t, block, p] = back_stage[t, block, p]

    def slots_in(t, block):
        others(side, p, lambda q: slot_copy(t, block, q, p).wait_recv())

    def forward(block):
        slots_in(0, block)
        inputs = inbox[0, block].reshape(width, latent)
        pre = dot(inputs, gate_ref[...], ROWS_COLS)
        raised = dot(inputs, up_ref[...], ROWS_COLS)
        gate_pre[block] = pre
        up_pre[block] = raised
        hidden = (pre * jax.nn.sigmoid(pre) * raised).astype(BF16)
        hid[block] = hidden
        hand_back(0, block, dot(hidden, down_ref[...], ROWS_COLS))

    def backward(block):
        pre, raised = gate_pre[block], up_pre[block]
        sig = jax.nn.sigmoid(pre)
        grads = inbox[1, block].reshape(width, latent)
        hidden_grad = dot(grads, down_ref[...], LAST_LAST)
        up_g = (hidden_grad * pre * sig).astype(BF16)
        gate_g = (hidden_grad * raised * sig * (1.0 + pre * (1.0 - sig))).astype(BF16)
        up_gp[block] = up_g
        gate_gp[block] = gate_g
        hand_back(
            1, block, dot(gate_g, gate_ref[...], LAST_LAST) + dot(up_g, up_ref[...], LAST_LAST)
        )

    def columns(j):
        return pl.ds(pl.multiple_of(j * share, share), share)

    def weight_part(kind, j):
        flat = lambda value: value.reshape(side * width, value.shape[-1])
        if kind == 2:
            return dot(flat(hid[...]), flat(inbox[1, :, :, :, columns(j)]), FIRST_FIRST).astype(BF16)
        grads = flat((gate_gp if kind == 0 else up_gp)[...])
        return dot(flat(inbox[0, :, :, :, columns(j)]), grads, FIRST_FIRST).astype(BF16)

    def share_out(kind):
        def one(j):
            (dp_gate, dp_up, dp_down)[kind][j] = weight_part(kind, j)
            dp_copy(kind, dp, j).start()
        others(nd, dp, one)

    def keep_own(kind):
        (dp_gate, dp_up, dp_down)[kind][dp] = weight_part(kind, dp)
        own_share(kind).start()

    def combine(t, block):
        others(side, p, lambda q: back_copy(t, block, q, p).wait_recv())
        hot, scaled = selector(block)
        values = back[t, block].reshape(width, latent)
        if t == 1:
            return dot(hot.astype(BF16), values, FIRST_FIRST)
        high = scaled.astype(BF16)
        low = (scaled - high.astype(F32)).astype(BF16)
        return dot(high, values, FIRST_FIRST) + dot(low, values, FIRST_FIRST)

    def pass_on(t, way, block, dst, has_prior):
        total = combine(t, block)

        @pl.when(has_prior)
        def _():
            hop_copy(t, way, block, z).wait_recv()
            part[t, block] = (total + hop[t, way, block].astype(F32)).astype(BF16)

        @pl.when(jnp.logical_not(has_prior))
        def _():
            part[t, block] = total.astype(BF16)

        hop_copy(t, way, block, dst).start()

    def wave(t, w):
        @pl.when(w >= z)
        def _():
            pass_on(t, 0, side - 1 - (w - z), z + 1, z > 0)

        @pl.when(w >= side - 1 - z)
        def _():
            pass_on(t, 1, w - (side - 1 - z), z - 1, z + 1 < side)

    def finish(t, out):
        out[...] = combine(t, z).astype(BF16)

        def add(way):
            hop_copy(t, way, z, z).wait_recv()
            out[...] = (out[...].astype(F32) + hop[t, way, z].astype(F32)).astype(BF16)

        @pl.when(z > 0)
        def _():
            add(0)

        @pl.when(z + 1 < side)
        def _():
            add(1)

    def token_step(d):
        arrive(0, d)

        @pl.when(d > 0)
        def _():
            @pl.when(d == 1)
            def _():
                for load in loads[2:]:
                    load.wait()
            visit(d - 1, forward)

    def grad_step(d):
        arrive(1, d)

        @pl.when(d == 0)
        def _():
            visit(side - 1, forward)

        @pl.when(d > 0)
        def _():
            visit(d - 1, lambda block: slots_in(1, block))
            visit(d - 1, backward)
            wave(0, d - 1)

    loop(0, side, token_step)
    loads[1].wait()
    loop(0, side, grad_step)
    visit(side - 1, lambda block: slots_in(1, block))
    visit(side - 1, backward)
    share_out(0)
    share_out(1)
    share_out(2)
    wave(1, 0)
    finish(0, mixed_ref)
    for w in range(1, side - 1):
        wave(1, w)
        if w <= 3:
            keep_own(w - 1)
    for kind in range(max(0, min(side - 2, 3)), 3):
        keep_own(kind)
    finish(1, lgrad_ref)

    for kind in range(3):
        others(nd, dp, lambda j: dp_copy(kind, j, dp).wait_recv())
        own_share(kind).wait()
        others(nd, dp, lambda j: dp_copy(kind, dp, j).wait_send())
    others(side, z, lambda k: meta_copy(z, k).wait_send())
    for t in range(2):
        def line_sent(block):
            @pl.when((block <= z) & (z + 1 < side))
            def _():
                line_copy(t, 0, block, z + 1).wait_send()

            @pl.when((block >= z) & (z > 0))
            def _():
                line_copy(t, 1, block, z - 1).wait_send()

            @pl.when(block > z)
            def _():
                hop_copy(t, 0, block, z + 1).wait_send()

            @pl.when(block < z)
            def _():
                hop_copy(t, 1, block, z - 1).wait_send()

            def plane_sent(q):
                slot_copy(t, block, p, q).wait_send()
                back_copy(t, block, p, q).wait_send()

            others(side, p, plane_sent)

        loop(0, side, line_sent)


def add_parts(mixed_ref, lgrad_ref, gate_parts, up_parts, down_parts, *outs):
    outs[0][...] = mixed_ref[...]
    outs[1][...] = lgrad_ref[...]
    for parts, out in zip((gate_parts, up_parts, down_parts), outs[2:]):
        out[0] = jnp.sum(parts[...].astype(F32), axis=0)


def shards(tokens, routes, route_weights, gate_weight, up_weight, down_weight, cotangent):
    rows, latent = tokens.shape
    top = routes.shape[1]
    ffn = gate_weight.shape[2]
    experts, nd = lax.axis_size("expert"), lax.axis_size("dp")
    side = math.isqrt(experts)
    assert side * side == experts
    capacity = rows * top // experts
    cap = -(-capacity // 16) * 16
    width, share = side * cap, latent // nd
    vmem = pl.BlockSpec(memory_space=pltpu.VMEM)
    hbm = pl.BlockSpec(memory_space=pl.ANY)
    dma = lambda *shape: pltpu.SemaphoreType.DMA(shape)
    row_out = jax.ShapeDtypeStruct((rows, latent), BF16)
    params = functools.partial(pltpu.CompilerParams, vmem_limit_bytes=60 * 1024 * 1024)
    parts = pl.pallas_call(
        functools.partial(kernel, side, nd, capacity, cap),
        out_shape=(
            row_out,
            row_out,
            jax.ShapeDtypeStruct((nd, share, ffn), BF16),
            jax.ShapeDtypeStruct((nd, share, ffn), BF16),
            jax.ShapeDtypeStruct((nd, ffn, share), BF16),
        ),
        in_specs=[vmem] * 2 + [hbm] * 5,
        out_specs=[vmem] * 2 + [hbm] * 3,
        scratch_shapes=[
            pltpu.VMEM((latent, ffn), BF16),
            pltpu.VMEM((latent, ffn), BF16),
            pltpu.VMEM((ffn, latent), BF16),
            pltpu.VMEM((side, 2 * experts, rows), F32),
            pltpu.VMEM((2, side, rows, latent), BF16),
            pltpu.VMEM((2, side, side, cap, latent), BF16),
            pltpu.VMEM((2, side, side, cap, latent), BF16),
            pltpu.VMEM((2, side, side, cap, latent), BF16),
            pltpu.VMEM((2, side, side, cap, latent), BF16),
            pltpu.VMEM((2, side, rows, latent), BF16),
            pltpu.VMEM((2, 2, side, rows, latent), BF16),
            pltpu.VMEM((side, width, ffn), F32),
            pltpu.VMEM((side, width, ffn), F32),
            pltpu.VMEM((side, width, ffn), BF16),
            pltpu.VMEM((side, width, ffn), BF16),
            pltpu.VMEM((side, width, ffn), BF16),
            pltpu.VMEM((nd, share, ffn), BF16),
            pltpu.VMEM((nd, share, ffn), BF16),
            pltpu.VMEM((nd, ffn, share), BF16),
            dma(5), dma(side), dma(side),
            dma(2, 2, side), dma(2, side),
            dma(2, side, side), dma(2, side, side),
            dma(2, side, side), dma(2, side, side),
            dma(2, 2, side), dma(2, 2, side),
            dma(3, nd), dma(3, nd),
        ],
        compiler_params=params(collective_id=0, has_side_effects=True),
    )(
        routes.T, route_weights.T, tokens, cotangent, gate_weight[0], up_weight[0], down_weight[0]
    )
    return pl.pallas_call(
        add_parts,
        out_shape=(
            row_out,
            row_out,
            jax.ShapeDtypeStruct((1, share, ffn), F32),
            jax.ShapeDtypeStruct((1, share, ffn), F32),
            jax.ShapeDtypeStruct((1, ffn, share), F32),
        ),
        in_specs=[vmem] * 5,
        out_specs=[vmem] * 5,
        compiler_params=params(),
    )(*parts)


def solution(mesh):
    rows = P(("dp", "expert"), None)
    per_expert = P("expert", None, None)
    return jax.shard_map(
        shards,
        mesh=mesh,
        in_specs=(rows, rows, rows, per_expert, per_expert, per_expert, rows),
        out_specs=(
            rows, rows, P("expert", "dp", None), P("expert", "dp", None), P("expert", None, "dp")
        ),
        check_vma=False,
    )
```

time: 129 us -> 115 us (0.89)
  local copies, waits for them, and re-layouts: 7.6 us -> 0 us
  Pallas kernels: 120 us -> 114 us
    pallas_call x1, Pallas kernels: 120 us -> 110 us  [shards(): pl.pallas_call(functools.partial(kernel, side, nd, capacity, cap), out_sh...]
    unnamed x11 -> x0, local copies, waits for them, and re-layouts: 7.6 us -> none
    pallas_call x0 -> x1, Pallas kernels: none -> 3.88 us  [shards(): pl.pallas_call(add_parts, out_shape=(row_out, row_out, jax.ShapeDtypeStru...]
where the time goes in v3:
time: 115 us
  Pallas kernels  114 us (99%)
    pallas_call x1, Pallas kernels, shards(): pl.pallas_call(functools.partial(kernel, side, nd, capacity, cap), out_sh...  110 us
    pallas_call x1, Pallas kernels, shards(): pl.pallas_call(add_parts, out_shape=(row_out, row_out, jax.ShapeDtypeStru...  3.88 us

profile of v3, /device:TPU:1, one launch (start us, length us, event | category | flops | bytes accessed | tf_op | source)
XLA Modules:
  0.0 114.9 jit_solution(9607466408374078595)
XLA Ops:
  0.6 110.4 %shard_map.110 = (bf16[128,1024]{1,0:T(8,128)(2,1)}, bf16[128,1024]{1,0:T(8,128)(2,1)}, bf16[2,512,512]{2,1,0:T(8,128)(2,1)}, bf16[2,512,512]{2,1,0:T(8,128)(2,1)}, bf16[2,512,512]{2,1,0:T(8,128)(2,1)}) custom-call(s32[6,128]{1,0:T(8,128)} %bitcast.8, f32[6,128]{1,0:T(8,128)} %bitcast.9, bf16[128,1024]{1,0:T(8,128)(2,1)} %tok_hbm.1, ...), custom_call_target="tpu_custom_call" | custom-call | tf_op jit(solution)/shard_map/pallas_call | solution.py:392
  111.0 3.9 %shard_map.111 = (bf16[128,1024]{1,0:T(8,128)(2,1)}, bf16[128,1024]{1,0:T(8,128)(2,1)}, f32[1,512,512]{2,1,0:T(8,128)}, f32[1,512,512]{2,1,0:T(8,128)}, f32[1,512,512]{2,1,0:T(8,128)}) custom-call(bf16[128,1024]{1,0:T(8,128)(2,1)} %get-tuple-element.10.mixed_ref, bf16[128,1024]{1,0:T(8,128)(2,1)} %get-tuple-element.11.lgrad_ref, ...), custom_call_target="tpu_custom_call" | custom-call | tf_op jit(solution)/shard_map/pallas_call | solution.py:434

commit v4 on v3

--- a/solution.py
+++ b/solution.py
@@ -25,10 +25,10 @@
     routes_ref, weights_ref, tok_hbm, cot_hbm, gate_hbm, up_hbm, down_hbm,
     mixed_ref, lgrad_ref, gate_parts, up_parts, down_parts,
     gate_ref, up_ref, down_ref,
-    meta, line, stage, inbox, back_stage, back, part, hop, gate_pre, up_pre, hid, gate_gp, up_gp,
+    meta, line, stage, inbox, back_stage, back, part, home, total, gate_pre, up_pre, hid, gate_gp, up_gp,
     dp_gate, dp_up, dp_down,
     load_sem, meta_send, meta_recv, line_send, line_recv, slot_send, slot_recv, back_send,
-    back_recv, hop_send, hop_recv, dp_send, dp_recv,
+    back_recv, home_send, home_recv, dp_send, dp_recv,
 ):
     experts = side * side
     top, rows = routes_ref.shape
@@ -117,10 +117,10 @@
             back_send.at[t, block, dst], back_recv.at[t, block, src], at_plane(dst),
         )
 
-    def hop_copy(t, way, block, dst):
+    def home_copy(t, src, dst):
         return remote(
-            part.at[t, block], hop.at[t, way, block], hop_send.at[t, way, block],
-            hop_recv.at[t, way, block], at_line(dst),
+            part.at[t, dst], home.at[t, src], home_send.at[t, dst], home_recv.at[t, src],
+            at_line(dst),
         )
 
     def dp_copy(kind, src, dst):
@@ -255,43 +255,21 @@
         low = (scaled - high.astype(F32)).astype(BF16)
         return dot(high, values, FIRST_FIRST) + dot(low, values, FIRST_FIRST)
 
-    def pass_on(t, way, block, dst, has_prior):
-        total = combine(t, block)
-
-        @pl.when(has_prior)
-        def _():
-            hop_copy(t, way, block, z).wait_recv()
-            part[t, block] = (total + hop[t, way, block].astype(F32)).astype(BF16)
-
-        @pl.when(jnp.logical_not(has_prior))
-        def _():
-            part[t, block] = total.astype(BF16)
-
-        hop_copy(t, way, block, dst).start()
-
-    def wave(t, w):
-        @pl.when(w >= z)
-        def _():
-            pass_on(t, 0, side - 1 - (w - z), z + 1, z > 0)
-
-        @pl.when(w >= side - 1 - z)
-        def _():
-            pass_on(t, 1, w - (side - 1 - z), z - 1, z + 1 < side)
+    def deliver(t, d):
+        def one(block):
+            part[t, block] = combine(t, block).astype(BF16)
+            home_copy(t, z, block).start()
+        visit(d, one)
 
     def finish(t, out):
-        out[...] = combine(t, z).astype(BF16)
-
-        def add(way):
-            hop_copy(t, way, z, z).wait_recv()
-            out[...] = (out[...].astype(F32) + hop[t, way, z].astype(F32)).astype(BF16)
-
-        @pl.when(z > 0)
-        def _():
-            add(0)
-
-        @pl.when(z + 1 < side)
-        def _():
-            add(1)
+        total[...] = combine(t, z)
+
+        def add(src):
+            home_copy(t, src, z).wait_recv()
+            total[...] += home[t, src].astype(F32)
+
+        others(side, z, add)
+        out[...] = total[...].astype(BF16)
 
     def token_step(d):
         arrive(0, d)
@@ -315,23 +293,19 @@
         def _():
             visit(d - 1, lambda block: slots_in(1, block))
             visit(d - 1, backward)
-            wave(0, d - 1)
+            deliver(0, d)
 
     loop(0, side, token_step)
     loads[1].wait()
     loop(0, side, grad_step)
     visit(side - 1, lambda block: slots_in(1, block))
+    share_out(2)
     visit(side - 1, backward)
     share_out(0)
     share_out(1)
-    share_out(2)
-    wave(1, 0)
+    loop(1, side, lambda d: deliver(1, d))
     finish(0, mixed_ref)
-    for w in range(1, side - 1):
-        wave(1, w)
-        if w <= 3:
-            keep_own(w - 1)
-    for kind in range(max(0, min(side - 2, 3)), 3):
+    for kind in (2, 0, 1):
         keep_own(kind)
     finish(1, lgrad_ref)
 
@@ -350,13 +324,9 @@
             def _():
                 line_copy(t, 1, block, z - 1).wait_send()
 
-            @pl.when(block > z)
-            def _():
-                hop_copy(t, 0, block, z + 1).wait_send()
-
-            @pl.when(block < z)
-            def _():
-                hop_copy(t, 1, block, z - 1).wait_send()
+            @pl.when(block != z)
+            def _():
+                home_copy(t, z, block).wait_send()
 
             def plane_sent(q):
                 slot_copy(t, block, p, q).wait_send()
@@ -411,7 +381,8 @@
             pltpu.VMEM((2, side, side, cap, latent), BF16),
             pltpu.VMEM((2, side, side, cap, latent), BF16),
             pltpu.VMEM((2, side, rows, latent), BF16),
-            pltpu.VMEM((2, 2, side, rows, latent), BF16),
+            pltpu.VMEM((2, side, rows, latent), BF16),
+            pltpu.VMEM((rows, latent), F32),
             pltpu.VMEM((side, width, ffn), F32),
             pltpu.VMEM((side, width, ffn), F32),
             pltpu.VMEM((side, width, ffn), BF16),
@@ -424,13 +395,14 @@
             dma(2, 2, side), dma(2, side),
             dma(2, side, side), dma(2, side, side),
             dma(2, side, side), dma(2, side, side),
-            dma(2, 2, side), dma(2, 2, side),
+            dma(2, side), dma(2, side),
             dma(3, nd), dma(3, nd),
         ],
         compiler_params=params(collective_id=0, has_side_effects=True),
     )(
         routes.T, route_weights.T, tokens, cotangent, gate_weight[0], up_weight[0], down_weight[0]
     )
+    steps = 4
     return pl.pallas_call(
         add_parts,
         out_shape=(
@@ -440,8 +412,21 @@
             jax.ShapeDtypeStruct((1, share, ffn), F32),
             jax.ShapeDtypeStruct((1, ffn, share), F32),
         ),
-        in_specs=[vmem] * 5,
-        out_specs=[vmem] * 5,
+        grid=(steps,),
+        in_specs=[
+            pl.BlockSpec((rows // steps, latent), lambda i: (i, 0)),
+            pl.BlockSpec((rows // steps, latent), lambda i: (i, 0)),
+            pl.BlockSpec((nd, share // steps, ffn), lambda i: (0, i, 0)),
+            pl.BlockSpec((nd, share // steps, ffn), lambda i: (0, i, 0)),
+            pl.BlockSpec((nd, ffn // steps, share), lambda i: (0, i, 0)),
+        ],
+        out_specs=[
+            pl.BlockSpec((rows // steps, latent), lambda i: (i, 0)),
+            pl.BlockSpec((rows // steps, latent), lambda i: (i, 0)),
+            pl.BlockSpec((1, share // steps, ffn), lambda i: (0, i, 0)),
+            pl.BlockSpec((1, share // steps, ffn), lambda i: (0, i, 0)),
+            pl.BlockSpec((1, ffn // steps, share), lambda i: (0, i, 0)),
+        ],
         compiler_params=params(),
     )(*parts)
 

time: 115 us -> 113 us (0.983)
    pallas_call x1, Pallas kernels: 110 us -> 108 us  [shards(): pl.pallas_call(functools.partial(kernel, side, nd, capacity, cap), out_sh...]
where the time goes in v4:
time: 113 us
  Pallas kernels  113 us (100%)
    pallas_call x1, Pallas kernels, shards(): pl.pallas_call(functools.partial(kernel, side, nd, capacity, cap), out_sh...  108 us
    pallas_call x1, Pallas kernels, shards(): pl.pallas_call(add_parts, out_shape=(row_out, row_out, jax.ShapeDtypeStru...  4.37 us

profile of v4, /device:TPU:1, one launch (start us, length us, event | category | flops | bytes accessed | tf_op | source)
XLA Modules:
  0.0 113.2 jit_solution(93322402079125462)
XLA Ops:
  0.6 108.2 %shard_map.110 = (bf16[128,1024]{1,0:T(8,128)(2,1)}, bf16[128,1024]{1,0:T(8,128)(2,1)}, bf16[2,512,512]{2,1,0:T(8,128)(2,1)}, bf16[2,512,512]{2,1,0:T(8,128)(2,1)}, bf16[2,512,512]{2,1,0:T(8,128)(2,1)}) custom-call(s32[6,128]{1,0:T(8,128)} %bitcast.8, f32[6,128]{1,0:T(8,128)} %bitcast.9, bf16[128,1024]{1,0:T(8,128)(2,1)} %tok_hbm.1, ...), custom_call_target="tpu_custom_call" | custom-call | tf_op jit(solution)/shard_map/pallas_call | solution.py:362
  108.8 4.4 %shard_map.111 = (bf16[128,1024]{1,0:T(8,128)(2,1)}, bf16[128,1024]{1,0:T(8,128)(2,1)}, f32[1,512,512]{2,1,0:T(8,128)}, f32[1,512,512]{2,1,0:T(8,128)}, f32[1,512,512]{2,1,0:T(8,128)}) custom-call(bf16[128,1024]{1,0:T(8,128)(2,1)} %get-tuple-element.10.mixed_ref, bf16[128,1024]{1,0:T(8,128)(2,1)} %get-tuple-element.11.lgrad_ref, ...), custom_call_target="tpu_custom_call" | custom-call | tf_op jit(solution)/shard_map/pallas_call | solution.py:406

commit v5 on v4

--- a/solution.py
+++ b/solution.py
@@ -94,6 +94,7 @@
     meta[z, 0:experts, :] = jnp.where(kept > 0.0, rank, -1.0)
     meta[z, experts : 2 * experts, :] = weight
     loads[0].wait()
+    loads[1].wait()
     pl.semaphore_wait(barrier, 2 * (side - 1) + nd - 1)
 
     def meta_copy(src, dst):
@@ -163,7 +164,7 @@
         others(side, p, lambda q: slot_copy(t, block, p, q).start())
         inbox[t, block, p] = stage[t, block, p]
 
-    def arrive(t, d):
+    def relay(t, d, start):
         def come(block):
             @pl.when(d > 0)
             def _():
@@ -175,7 +176,7 @@
         def _():
             come(z - d)
 
-            @pl.when(z + 1 < side)
+            @pl.when((z + 1 < side) & start)
             def _():
                 line_copy(t, 0, z - d, z + 1).start()
 
@@ -183,10 +184,12 @@
         def _():
             come(z + d)
 
-            @pl.when(z > 0)
+            @pl.when((z > 0) & start)
             def _():
                 line_copy(t, 1, z + d, z - 1).start()
 
+    def arrive(t, d):
+        relay(t, d, True if t == 0 else d > 0)
         if t == 0:
             @pl.when(d == 0)
             def _():
@@ -271,38 +274,47 @@
         others(side, z, add)
         out[...] = total[...].astype(BF16)
 
+    def backward_at(d):
+        visit(d, lambda block: slots_in(1, block))
+        visit(d, backward)
+
     def token_step(d):
+        @pl.when(d == side - 1)
+        def _():
+            relay(1, 0, True)
+
         arrive(0, d)
 
-        @pl.when(d > 0)
-        def _():
-            @pl.when(d == 1)
-            def _():
-                for load in loads[2:]:
-                    load.wait()
-            visit(d - 1, forward)
+        @pl.when(d == 2)
+        def _():
+            for load in loads[2:]:
+                load.wait()
+
+        @pl.when(d >= 2)
+        def _():
+            visit(d - 2, forward)
 
     def grad_step(d):
         arrive(1, d)
 
-        @pl.when(d == 0)
-        def _():
-            visit(side - 1, forward)
-
-        @pl.when(d > 0)
-        def _():
-            visit(d - 1, lambda block: slots_in(1, block))
-            visit(d - 1, backward)
-            deliver(0, d)
+        @pl.when(d < 2)
+        def _():
+            visit(side - 2 + d, forward)
+
+        @pl.when(d >= 2)
+        def _():
+            backward_at(d - 2)
+            deliver(0, d - 1)
 
     loop(0, side, token_step)
-    loads[1].wait()
     loop(0, side, grad_step)
+    backward_at(side - 2)
     visit(side - 1, lambda block: slots_in(1, block))
     share_out(2)
     visit(side - 1, backward)
     share_out(0)
     share_out(1)
+    deliver(0, side - 1)
     loop(1, side, lambda d: deliver(1, d))
     finish(0, mixed_ref)
     for kind in (2, 0, 1):
@@ -402,7 +414,6 @@
     )(
         routes.T, route_weights.T, tokens, cotangent, gate_weight[0], up_weight[0], down_weight[0]
     )
-    steps = 4
     return pl.pallas_call(
         add_parts,
         out_shape=(
@@ -412,21 +423,8 @@
             jax.ShapeDtypeStruct((1, share, ffn), F32),
             jax.ShapeDtypeStruct((1, ffn, share), F32),
         ),
-        grid=(steps,),
-        in_specs=[
-            pl.BlockSpec((rows // steps, latent), lambda i: (i, 0)),
-            pl.BlockSpec((rows // steps, latent), lambda i: (i, 0)),
-            pl.BlockSpec((nd, share // steps, ffn), lambda i: (0, i, 0)),
-            pl.BlockSpec((nd, share // steps, ffn), lambda i: (0, i, 0)),
-            pl.BlockSpec((nd, ffn // steps, share), lambda i: (0, i, 0)),
-        ],
-        out_specs=[
-            pl.BlockSpec((rows // steps, latent), lambda i: (i, 0)),
-            pl.BlockSpec((rows // steps, latent), lambda i: (i, 0)),
-            pl.BlockSpec((1, share // steps, ffn), lambda i: (0, i, 0)),
-            pl.BlockSpec((1, share // steps, ffn), lambda i: (0, i, 0)),
-            pl.BlockSpec((1, ffn // steps, share), lambda i: (0, i, 0)),
-        ],
+        in_specs=[vmem] * 5,
+        out_specs=[vmem] * 5,
         compiler_params=params(),
     )(*parts)
 

time: 113 us -> 112 us (level)
  Pallas kernels: 113 us -> 111 us
where the time goes in v5:
time: 112 us
  Pallas kernels  111 us (99%)
    pallas_call x1, Pallas kernels, shards(): pl.pallas_call(functools.partial(kernel, side, nd, capacity, cap), out_sh...  107 us
    pallas_call x1, Pallas kernels, shards(): pl.pallas_call(add_parts, out_shape=(row_out, row_out, jax.ShapeDtypeStru...  3.88 us

profile of v5, /device:TPU:1, one launch (start us, length us, event | category | flops | bytes accessed | tf_op | source)
XLA Modules:
  0.0 111.8 jit_solution(15371159447056324339)
XLA Ops:
  0.6 107.3 %shard_map.110 = (bf16[128,1024]{1,0:T(8,128)(2,1)}, bf16[128,1024]{1,0:T(8,128)(2,1)}, bf16[2,512,512]{2,1,0:T(8,128)(2,1)}, bf16[2,512,512]{2,1,0:T(8,128)(2,1)}, bf16[2,512,512]{2,1,0:T(8,128)(2,1)}) custom-call(s32[6,128]{1,0:T(8,128)} %bitcast.8, f32[6,128]{1,0:T(8,128)} %bitcast.9, bf16[128,1024]{1,0:T(8,128)(2,1)} %tok_hbm.1, ...), custom_call_target="tpu_custom_call" | custom-call | tf_op jit(solution)/shard_map/pallas_call | solution.py:374
  107.9 3.9 %shard_map.111 = (bf16[128,1024]{1,0:T(8,128)(2,1)}, bf16[128,1024]{1,0:T(8,128)(2,1)}, f32[1,512,512]{2,1,0:T(8,128)}, f32[1,512,512]{2,1,0:T(8,128)}, f32[1,512,512]{2,1,0:T(8,128)}) custom-call(bf16[128,1024]{1,0:T(8,128)(2,1)} %get-tuple-element.10.mixed_ref, bf16[128,1024]{1,0:T(8,128)(2,1)} %get-tuple-element.11.lgrad_ref, ...), custom_call_target="tpu_custom_call" | custom-call | tf_op jit(solution)/shard_map/pallas_call | solution.py:417
